TPU v7x, 256 devices: a whole 4x4x8 slice. The times are simulated.
256 devices in a mesh: pair: 32 (over z, y), virt: 8 (over x, core).
Axes of the slice: x: 4, y: 4, z: 8, core: 2. Of those that a mesh axis runs over, the one named last changes fastest.
Arguments:
- amplitudes: bfloat16 [16384, 9216], P('pair', 'virt'), may hold values from -6 to 6
- block_mask: int32 [16384, 4], P('pair'), may hold values from 0 to 1, as said below
- integrals: bfloat16 [9216, 9216], P('pair', 'virt'), may hold values from -0.0625 to 0.0625
- mirror: int32 [16384], P('pair'), may hold values from 0 to 16383, as said below
Outputs:
- residual: bfloat16 [16384, 9216], P('pair', 'virt')
Inputs may be any that keep to these rules, and one draw needn't show every extreme that they name: mirror is an involution without fixed points; the pair at local row d * 16 + s of pair index p has its mirror on pair index d, at a local row from p * (16) to p * 16 + 512 // 32 - 1. block_mask[g, 2 * t + u] equals block_mask[mirror[g], 2 * u + t]; every pair has at least one active tile pair.
All inputs are finite; a program needn't handle non-finite values.
Results may differ from a plain program's by a relative error of at most 0.0051.
Values may be sent and summed in bfloat16 or wider, within the bound.
No kernel may reach another device: no remote copies, remote signals or barrier semaphores. Data moves between devices by JAX's collectives and lax.ppermute only.
A program may use at most 192 MiB of HBM per device.

v0:
```python
import jax
import jax.numpy as jnp
from jax import lax
from jax.sharding import PartitionSpec as P

TW = 48
NTILE = 2
V = 96
NBLK = 4


def tile_live(block_mask, width):
    virt_count = lax.axis_size("virt")
    virt_index = lax.axis_index("virt")
    a_block = V // virt_count
    column = jnp.arange(width, dtype=jnp.int32)
    first_virtual = virt_index * a_block + column // V
    second_virtual = column % V
    tile_pair = first_virtual // TW * NTILE + second_virtual // TW
    one_hot = (tile_pair[None, :] == jnp.arange(NBLK, dtype=jnp.int32)[:, None]).astype(jnp.float32)
    counted = jnp.dot(block_mask.astype(jnp.float32), one_hot, precision=lax.Precision.HIGHEST)
    return counted > 0.5


def local(amplitudes, block_mask, integrals, mirror):
    pair_rows, width = amplitudes.shape
    pair_count = lax.axis_size("pair")
    virt_count = lax.axis_size("virt")
    pair_index = lax.axis_index("pair")
    a_block = V // virt_count
    live = tile_live(block_mask, width)
    masked = jnp.where(live, amplitudes, jnp.zeros_like(amplitudes))
    all_columns = lax.all_gather(masked, "virt", axis=1, tiled=True)
    whole = lax.all_gather(integrals, "pair", axis=0, tiled=True)
    ladder = jnp.dot(all_columns, whole, preferred_element_type=jnp.float32)
    direct = ladder.astype(jnp.bfloat16)
    slot_rows = pair_rows // pair_count
    arranged = direct.reshape(pair_count, slot_rows, a_block, virt_count, a_block)
    arranged = jnp.transpose(arranged, (3, 0, 1, 2, 4)).reshape(
        virt_count, pair_count, slot_rows * a_block * a_block
    )
    halfway = lax.all_to_all(arranged, "pair", split_axis=1, concat_axis=1, tiled=True)
    received = lax.all_to_all(halfway, "virt", split_axis=0, concat_axis=0, tiled=True)
    received = received.reshape(virt_count, pair_count, slot_rows, a_block, a_block)
    received = jnp.transpose(received, (1, 2, 4, 0, 3)).reshape(pair_count * slot_rows, width)
    source = mirror // pair_rows
    position = source * slot_rows + mirror % pair_rows - pair_index * slot_rows
    mirrored = jnp.take(received, position, axis=0)
    total = direct.astype(jnp.float32) + mirrored.astype(jnp.float32)
    return jnp.where(live, total, jnp.zeros_like(total)).astype(jnp.bfloat16)


def solution(mesh):
    in_specs = (P("pair", "virt"), P("pair", None), P("pair", "virt"), P("pair"))
    out_specs = P("pair", "virt")
    return jax.shard_map(local, mesh=mesh, in_specs=in_specs, out_specs=out_specs, check_vma=False)
```

profile of v0, /device:TPU:8, one launch (start us, length us, event | category | flops | bytes accessed | tf_op | source)
XLA Modules:
  0.0 387.0 jit_solution(13815038097259881634)
XLA Ops:
  6.5 0.0 all-gather.3.cloned.1.call-start
  6.5 0.0 copy-start.1
  6.5 1.6 copy.16
  8.2 0.0 copy-done.1
  8.2 2.7 broadcast_select_fusion
  10.9 0.0 all-gather.3.cloned.1.call-update
  10.9 0.0 all-gather.5.cloned.1.call-start
  11.0 0.7 all-gather.5.cloned.1.call-update
  11.7 58.9 %all-gather.3.cloned.1.call-done = bf16[512,9216]{0,1:T(8,128)(2,1)} async-done(((bf16[512,1152]{0,1:T(8,128)(2,1)}), bf16[512,9216]{0,1:T(8,128)(2,1)}) %all-gather.3.cloned.1.call-update) | async-done | bytes 9437200 | tf_op jit(solution)/shard_map/all_gather | solution.py:33
  70.6 164.0 %all-gather.5.cloned.1.call-done = bf16[9216,1152]{1,0:T(8,128)(2,1)} async-done(((bf16[288,1152]{1,0:T(8,128)(2,1)}), bf16[9216,1152]{1,0:T(8,128)(2,1)}) %all-gather.5.cloned.1.call-update) | async-done | bytes 21233680 | tf_op jit(solution)/shard_map/all_gather | solution.py:34
  234.6 17.0 %convolution_convert_fusion = bf16[512,1152]{0,1:T(8,128)(2,1)S(1)} fusion(bf16[512,9216]{0,1:T(8,128)(2,1)} %all-gather.3.cloned.1.call-done, bf16[9216,1152]{1,0:T(8,128)(2,1)} %all-gather.5.cloned.1.call-done), kind=kOutput, calls=%fused_computation.2 | convolution fusion | flops 10872225792 | bytes 31850496 | tf_op jit(solution)/shard_map/dot_general | solution.py:35
  251.7 9.1 %reshape.53 = bf16[32,16,12,8,12]{1,0,4,3,2:T(8,128)(2,1)} reshape(bf16[512,1152]{0,1:T(8,128)(2,1)S(1)} %convolution_convert_fusion) | data formatting | bytes 2359296 | tf_op jit(solution)/shard_map/reshape | solution.py:38
  260.8 12.1 %copy.18 = bf16[8,32,16,12,12]{1,0,4,3,2:T(8,128)(2,1)} copy(bf16[8,32,16,12,12]{2,1,4,0,3:T(8,128)(2,1)} %bitcast.15) | data formatting | bytes 2359296 | tf_op jit(solution)/shard_map/transpose | solution.py:39
  272.9 6.3 %copy.19 = bf16[8,32,2304]{2,0,1:T(8,128)(2,1)S(1)} copy(bf16[8,32,2304]{1,0,2:T(8,128)(2,1)} %bitcast.16) | data formatting | bytes 2359296 | tf_op jit(solution)/shard_map/reshape | solution.py:39
  279.3 37.7 %all_to_all.10 = bf16[8,32,2304]{2,0,1:T(8,128)(2,1)S(1)} all-to-all(bf16[8,32,2304]{2,0,1:T(8,128)(2,1)S(1)} %copy.19), channel_id=1, replica_groups=mesh['pair'=32,'virt'=8] {'pair'}, dimensions={1} | all-to-all | bytes 2359296 | tf_op jit(solution)/shard_map/all_to_all | solution.py:42
  317.0 1.2 copy.20
  318.2 0.0 copy-start
  318.2 4.4 %all-to-all-start.1 = ((bf16[8,32,2304]{2,1,0:T(8,128)(2,1)}), bf16[8,32,2304]{2,1,0:T(8,128)(2,1)S(1)}, u32[]{:S(2)}, u32[]{:S(2)}) async-start(bf16[8,32,2304]{2,1,0:T(8,128)(2,1)} %copy.20), calls=%async_computation.1 | async-start | bytes 2359296 | tf_op jit(solution)/shard_map/all_to_all | solution.py:43
  322.6 0.0 copy-done
  322.6 17.3 %all-to-all-done.1 = bf16[8,32,2304]{2,1,0:T(8,128)(2,1)S(1)} async-done(((bf16[8,32,2304]{2,1,0:T(8,128)(2,1)}), bf16[8,32,2304]{2,1,0:T(8,128)(2,1)S(1)}, u32[]{:S(2)}, u32[]{:S(2)}) %all-to-all-start.1) | async-done | bytes 1179680 | tf_op jit(solution)/shard_map/all_to_all | solution.py:43
  340.0 5.0 %copy.21 = bf16[8,32,2304]{1,0,2:T(8,128)(2,1)} copy(bf16[8,32,2304]{2,1,0:T(8,128)(2,1)S(1)} %all-to-all-done.1) | data formatting | bytes 2359296 | tf_op jit(solution)/shard_map/all_to_all | solution.py:43
  345.0 12.5 %copy.22 = bf16[32,16,12,8,12]{1,0,4,3,2:T(8,128)(2,1)} copy(bf16[32,16,12,8,12]{0,3,2,4,1:T(8,128)(2,1)} %bitcast.17) | data formatting | bytes 2359296 | tf_op jit(solution)/shard_map/transpose | solution.py:45
  357.4 16.1 %reshape.56 = bf16[512,1152]{0,1:T(8,128)(2,1)S(1)} reshape(bf16[32,16,12,8,12]{1,0,4,3,2:T(8,128)(2,1)} %copy.22) | data formatting | bytes 2359296 | tf_op jit(solution)/shard_map/reshape | solution.py:45
  373.5 0.7 copy.23
  374.2 2.1 gather_fusion
  376.4 0.6 copy.24
  377.0 1.8 select_convert_fusion
  378.8 1.4 copy.25
  (3 shorter events, 0.0 us)
Async XLA Ops:
  6.5 64.1 %all-gather.3.cloned.1.call-start = ((), (), s32[]{:S(2)}) async-start(), calls=%async_computation.2 | async-start | bytes 10616832 | tf_op jit(solution)/shard_map/all_gather | solution.py:33
  6.5 1.6 copy-start.1
  10.9 223.7 %all-gather.5.cloned.1.call-start = ((), (), s32[]{:S(2)}) async-start(), calls=%async_computation.3 | async-start | bytes 21897216 | tf_op jit(solution)/shard_map/all_gather | solution.py:34
  318.2 4.4 %copy-start = (s32[512]{0:T(512)S(1)}, s32[512]{0:T(512)}, u32[]{:S(2)}) copy-start(s32[512]{0:T(512)} %param.7) | copy-start | bytes 6148
  318.2 21.8 %all-to-all-start.1 = ((bf16[8,32,2304]{2,1,0:T(8,128)(2,1)}), bf16[8,32,2304]{2,1,0:T(8,128)(2,1)S(1)}, u32[]{:S(2)}, u32[]{:S(2)}) async-start(bf16[8,32,2304]{2,1,0:T(8,128)(2,1)} %copy.20), calls=%async_computation.1 | async-start | bytes 2359296 | tf_op jit(solution)/shard_map/all_to_all | solution.py:43
Sparse Core Ops, SparseCore 0:
  11.1 59.5 all-gather.2
  73.2 161.3 all-gather.4
where the time goes:
time: 390 us; the launch traced here: 387 us
  waiting for transfers between devices  241 us (62%)
  local copies, waits for them, and re-layouts  68.8 us (18%)
  blocking collectives  37.7 us (10%)
  matrix products  19.8 us (5%)
  between operations  13.5 us (3%)
  starting transfers between devices  4.43 us (1%)
    all_gather x1, waiting for transfers between devices, local(): whole = lax.all_gather(integrals, 'pair', axis=0, tiled=True)  164 us
    all_gather x1, waiting for transfers between devices, local(): all_columns = lax.all_gather(masked, 'virt', axis=1, tiled=True)  58.9 us
    all_to_all x1, blocking collectives, local(): lax.all_to_all(arranged, 'pair', split_axis=1, concat_axis=1, tiled=True)  37.7 us
    all_to_all x1, waiting for transfers between devices, local(): lax.all_to_all(halfway, 'virt', split_axis=0, concat_axis=0, tiled=True)  17.3 us
    dot_general x1, matrix products, local(): ladder = jnp.dot(all_columns, whole, preferred_element_type=jnp.float32)  17 us
    reshape x2, local copies, waits for them, and re-layouts, local(): jnp.transpose(received, (1, 2, 4, 0, 3))  16.8 us
    transpose x1, local copies, waits for them, and re-layouts, local(): jnp.transpose(received, (1, 2, 4, 0, 3))  12.5 us
    transpose x1, local copies, waits for them, and re-layouts, local(): jnp.transpose(arranged, (3, 0, 1, 2, 4))  12.1 us
  transfers between devices with their start and end apart: 3, of which 3 were waited for; matrix products, arithmetic and copies ran while one was open for 0% of the time, Pallas kernels for 0%

commit v1 on v0

v1 whole, which is shorter than its diff:
```python
import functools

import jax
import jax.numpy as jnp
from jax import lax
from jax.experimental import pallas as pl
from jax.experimental.pallas import tpu as pltpu
from jax.sharding import Mesh, PartitionSpec as P

TW = 48
V = 96
Z, Y, X, C = 8, 4, 4, 2
VIRT = X * C
PAIR = Z * Y
A_BLOCK = V // VIRT
ROWS = 512
WIDTH = A_BLOCK * V
DEPTH = 288
SLOT = ROWS // PAIR
PIECE = A_BLOCK * A_BLOCK


def shift(axis, by):
    n = {"z": Z, "y": Y, "x": X, "c": C}[axis]
    return [(i, (i + by) % n) for i in range(n)]


def product_kernel(where_ref, *refs):
    blocks, b_ref, o_ref, a_ref = refs[:VIRT], refs[VIRT], refs[VIRT + 1], refs[VIRT + 2]
    for k, block in enumerate(blocks):
        at = pl.multiple_of(where_ref[k] * DEPTH, 16)
        a_ref[pl.ds(at, DEPTH), :] = block[0]
    o_ref[0] = lax.dot_general(
        a_ref[...], b_ref[...], (((0,), (0,)), ((), ())), preferred_element_type=jnp.float32
    ).astype(o_ref.dtype)


def product(where, blocks, b):
    groups, depth, rows = blocks[0].shape
    step = 256
    parts = rows // step
    a_spec = pl.BlockSpec((1, depth, step), lambda i, w: (i // parts, 0, i % parts))
    return pl.pallas_call(
        product_kernel,
        grid_spec=pltpu.PrefetchScalarGridSpec(
            num_scalar_prefetch=1,
            grid=(groups * parts,),
            in_specs=[a_spec] * VIRT + [pl.BlockSpec((VIRT * depth, WIDTH), lambda i, w: (0, 0))],
            out_specs=pl.BlockSpec((1, step, WIDTH), lambda i, w: (i // parts, i % parts, 0)),
            scratch_shapes=[pltpu.VMEM((VIRT * depth, step), jnp.bfloat16)],
        ),
        out_shape=jax.ShapeDtypeStruct((groups, rows, WIDTH), jnp.bfloat16),
        compiler_params=pltpu.CompilerParams(vmem_limit_bytes=48 * 2**20),
    )(where, *blocks, b)


def gather_x(block):
    half = block.shape[0] // 2
    left = lax.ppermute(block, "x", shift("x", 1))
    right = lax.ppermute(block, "x", shift("x", -1))
    far_low = lax.ppermute(left[:half], "x", shift("x", 1))
    far_high = lax.ppermute(right[half:], "x", shift("x", -1))
    return [block, left, right, jnp.concatenate([far_low, far_high], axis=0)]


def local(amplitudes, block_mask, integrals, mirror):
    z, y, x, c = (lax.axis_index(n) for n in "zyxc")
    virt = x * C + c
    pair = z * Y + y
    tile = virt * A_BLOCK // TW
    active = lax.dynamic_slice(block_mask, (0, 2 * tile), (ROWS, 2)) > 0
    column = jnp.arange(WIDTH, dtype=jnp.int32)
    first = (column % V) < TW
    live = jnp.where(first[None, :], active[:, :1], active[:, 1:])

    whole = lax.all_gather(integrals, "z", axis=0, tiled=True)

    masked = jnp.where(live, amplitudes, jnp.zeros_like(amplitudes))
    turned = masked.T.reshape(Y, DEPTH, ROWS)
    mine = lax.all_to_all(turned, "y", split_axis=0, concat_axis=0, tiled=True)
    along = gather_x(mine)
    across = [lax.ppermute(b, "c", shift("c", 1)) for b in along]
    order = [(x + d) % X for d in (0, -1, 1, 2)]
    where = jnp.stack([o * C + c for o in order] + [o * C + 1 - c for o in order]).astype(jnp.int32)
    partial = product(where, along + across, whole)

    direct = lax.psum_scatter(partial, "y", scatter_dimension=0, tiled=False)

    received = lax.all_to_all(direct.reshape(PAIR, SLOT, WIDTH), ("z", "y"), split_axis=0, concat_axis=0, tiled=True)
    received = received.reshape(ROWS, WIDTH)
    position = mirror // ROWS * SLOT + mirror % ROWS - pair * SLOT
    row = jnp.arange(ROWS, dtype=jnp.int32)
    pick = (position[:, None] == row[None, :]).astype(jnp.bfloat16)
    picked = jnp.dot(pick, received, preferred_element_type=jnp.float32).astype(jnp.bfloat16)
    outer, middle, inner = column // PIECE, column % PIECE // A_BLOCK, column % A_BLOCK
    send = ((inner * V + outer * A_BLOCK + middle)[:, None] == column[None, :]).astype(jnp.bfloat16)
    split = lax.dot_general(
        send, picked, (((1,), (1,)), ((), ())), preferred_element_type=jnp.float32
    ).astype(jnp.bfloat16)
    swapped = lax.all_to_all(split.reshape(VIRT, PIECE, ROWS), ("x", "c"), split_axis=0, concat_axis=0, tiled=True)
    swapped = swapped.reshape(WIDTH, ROWS)
    land = ((middle * V + outer * A_BLOCK + inner)[:, None] == column[None, :]).astype(jnp.bfloat16)
    mirrored = lax.dot_general(swapped, land, (((0,), (0,)), ((), ())), preferred_element_type=jnp.float32)
    total = direct.astype(jnp.float32) + mirrored
    return jnp.where(live, total, jnp.zeros_like(total)).astype(jnp.bfloat16)


def solution(mesh):
    grid = Mesh(mesh.devices.reshape(Z, Y, X, C), ("z", "y", "x", "c"))
    rows, columns = ("z", "y"), ("x", "c")
    in_specs = (P(rows, columns), P(rows, None), P(rows, columns), P(rows))
    return jax.shard_map(local, mesh=grid, in_specs=in_specs, out_specs=P(rows, columns), check_vma=False)
```

time: 390 us -> 227 us (0.58)
  waiting for transfers between devices: 241 us -> 141 us
  local copies, waits for them, and re-layouts: 68.8 us -> 2.52 us
  Pallas kernels: 0 us -> 19.4 us
  blocking collectives: 37.7 us -> 19.8 us
  starting transfers between devices: 4.43 us -> 21.6 us
  matrix products: 19.8 us -> 6.64 us
    all_gather x2 -> x1, waiting for transfers between devices: 223 us -> 0.01 us  [local(): whole = lax.all_gather(integrals, 'z', axis=0, tiled=True)]
    reduce_scatter x0 -> x1, waiting for transfers between devices: none -> 53.4 us  [local(): direct = lax.psum_scatter(partial, 'y', scatter_dimension=0, tiled=False)]
    ppermute x0 -> x8, waiting for transfers between devices: none -> 38.2 us  [the longest x1 24.6 us: gather_x(): left = lax.ppermute(block, 'x', shift('x', 1))]
    reshape x4 -> x0, local copies, waits for them, and re-layouts: 32.3 us -> none  [the longest x2 16.8 us: local(): jnp.transpose(received, (1, 2, 4, 0, 3))]
    all_to_all x1 -> x2, waiting for transfers between devices: 17.3 us -> 48.2 us  [the longest x1 30.9 us: local(): lax.all_to_all(direct.reshape(PAIR, SLOT, WIDTH), ('z', 'y'), split_axis=...]
    transpose x2 -> x1, local copies, waits for them, and re-layouts: 24.6 us -> 0.62 us  [local(): turned = masked.T.reshape(Y, DEPTH, ROWS)]
    pallas_call x0 -> x1, Pallas kernels: none -> 19.4 us  [product(): pl.pallas_call(product_kernel, grid_spec=pltpu.PrefetchScalarGridSpec(num...]
    all_to_all x1, blocking collectives: 37.7 us -> 19.8 us  [local(): mine = lax.all_to_all(turned, 'y', split_axis=0, concat_axis=0, tiled=True)]
  transfers between devices with their start and end apart: 3 -> 12, of which waited for: 3 -> 6; matrix products, arithmetic and copies ran while one was open for 0% -> 2% of each run, Pallas kernels for 0% -> 0%
where the time goes in v1:
time: 227 us
  waiting for transfers between devices  141 us (62%)
  starting transfers between devices  21.6 us (10%)
  blocking collectives  19.8 us (9%)
  Pallas kernels  19.4 us (9%)
  between operations  13.5 us (6%)
  matrix products  6.64 us (3%)
  other arithmetic  2.54 us (1%)
  local copies, waits for them, and re-layouts  2.52 us (1%)
    reduce_scatter x1, waiting for transfers between devices, local(): direct = lax.psum_scatter(partial, 'y', scatter_dimension=0, tiled=False)  53.4 us
    all_to_all x1, waiting for transfers between devices, local(): lax.all_to_all(direct.reshape(PAIR, SLOT, WIDTH), ('z', 'y'), split_axis=...  30.9 us
    ppermute x1, waiting for transfers between devices, gather_x(): left = lax.ppermute(block, 'x', shift('x', 1))  24.6 us
    all_to_all x1, blocking collectives, local(): mine = lax.all_to_all(turned, 'y', split_axis=0, concat_axis=0, tiled=True)  19.8 us
    pallas_call x1, Pallas kernels, product(): pl.pallas_call(product_kernel, grid_spec=pltpu.PrefetchScalarGridSpec(num...  19.4 us
    all_to_all x1, waiting for transfers between devices, local(): lax.all_to_all(split.reshape(VIRT, PIECE, ROWS), ('x', 'c'), split_axis=0...  17.3 us
    ppermute x1, waiting for transfers between devices, gather_x(): far_low = lax.ppermute(left[:half], 'x', shift('x', 1))  10.5 us
    all_to_all x1, starting transfers between devices, local(): lax.all_to_all(direct.reshape(PAIR, SLOT, WIDTH), ('z', 'y'), split_axis=...  10 us
  transfers between devices with their start and end apart: 12, of which 6 were waited for; matrix products, arithmetic and copies ran while one was open for 2% of the time, Pallas kernels for 0%

profile of v1, /device:TPU:8, one launch (start us, length us, event | category | flops | bytes accessed | tf_op | source)
XLA Modules:
  0.0 226.5 jit_solution(18299239089723529482)
XLA Ops:
  6.5 0.7 all-gather.2.cloned.1.call-update
  7.3 0.0 reduce-scatter.2.cloned.1.call-start
  7.4 0.7 dynamic-slice_compare_fusion
  8.1 1.8 fusion.6
  9.9 0.6 copy.5
  10.5 19.8 %all_to_all.15.refs_0_ = bf16[4,288,512]{2,1,0:T(8,128)(2,1)S(1)} all-to-all(bf16[4,288,512]{2,1,0:T(8,128)(2,1)S(1)} %bitcast.20), channel_id=1, replica_groups=mesh['z'=8,'y'=4,'x'=4,'c'=2] {'y'}, dimensions={0} | all-to-all | bytes 2359296 | tf_op jit(solution)/shard_map/all_to_all | solution.py:80
  30.2 1.5 collective-permute-start
  31.7 1.7 collective-permute-start.1
  33.5 24.6 %collective-permute-done.refs_1_ = bf16[4,288,512]{2,1,0:T(8,128)(2,1)S(1)} collective-permute-done((bf16[4,288,512]{2,1,0:T(8,128)(2,1)S(1)}, bf16[4,288,512]{2,1,0:T(8,128)(2,1)S(1)}, u32[]{:S(2)}, u32[]{:S(2)}) %collective-permute-start) | collective-permute-done | bytes 1179680 | tf_op jit(solution)/shard_map/ppermute | solution.py:59
  58.1 0.4 collective-permute-start.2
  58.5 0.0 collective-permute-done.1.refs_2_
  58.5 3.0 %collective-permute-start.3 = (bf16[2,288,512]{2,1,0:T(8,128)(2,1)S(1)}, bf16[2,288,512]{2,1,0:T(8,128)(2,1)S(1)}, u32[]{:S(2)}, u32[]{:S(2)}) collective-permute-start(bf16[2,288,512]{2,1,0:T(8,128)(2,1)S(1)} %slice.19), channel_id=1, source_target_pairs={{0,6},{2,0},{4,2},{6,4},{1,7},{3,1},{5,3},{7,5},{8,14},{10,8},{12,... | collective-permute-start | bytes 1769480 | tf_op jit(solution)/shard_map/ppermute | solution.py:62
  61.6 0.0 collective-permute-start.4
  61.6 0.5 collective-permute-start.5
  62.1 0.0 collective-permute-start.6
  62.1 10.5 %collective-permute-done.2 = bf16[2,288,512]{2,1,0:T(8,128)(2,1)S(1)} collective-permute-done((bf16[2,288,512]{2,1,0:T(8,128)(2,1)S(1)}, bf16[2,288,512]{2,1,0:T(8,128)(2,1)S(1)}, u32[]{:S(2)}, u32[]{:S(2)}) %collective-permute-start.2) | collective-permute-done | bytes 589856 | tf_op jit(solution)/shard_map/ppermute | solution.py:61
  72.6 0.9 constant_dynamic-update-slice_fusion.1
  73.4 0.0 collective-permute-done.3
  73.4 0.9 constant_dynamic-update-slice_fusion.refs_3_
  74.3 0.1 stack.35.where_ref
  74.4 0.0 collective-permute-done.4.refs_4_
  74.4 0.0 collective-permute-done.5.refs_5_
  74.4 3.1 %collective-permute-done.7.refs_7_ = bf16[4,288,512]{2,1,0:T(8,128)(2,1)} collective-permute-done((bf16[4,288,512]{2,1,0:T(8,128)(2,1)}, bf16[4,288,512]{2,1,0:T(8,128)(2,1)}, u32[]{:S(2)}, u32[]{:S(2)}) %collective-permute-start.7) | collective-permute-done | bytes 1179680 | tf_op jit(solution)/shard_map/ppermute | solution.py:82
  77.5 19.4 %shard_map.46 = bf16[4,512,1152]{2,1,0:T(8,128)(2,1)} custom-call(s32[8]{0:T(128)S(1)} %stack.35.where_ref, bf16[4,288,512]{2,1,0:T(8,128)(2,1)S(1)} %all_to_all.15.refs_0_, bf16[4,288,512]{2,1,0:T(8,128)(2,1)S(1)} %collective-permute-done.refs_1_, bf16[4,288,512]{2,1,0:T(8,128)(2,1)S(1)} %collective-permute-done.1.refs_2_, ...), custom_call_target="tpu_custom_call" | custom-call | tf_op jit(solution)/shard_map/pallas_call | solution.py:43
  96.9 0.0 reduce-scatter.2.cloned.1.call-update
  96.9 53.4 %reduce-scatter.2.cloned.1.call-done = bf16[1,512,1152]{2,1,0:T(8,128)(2,1)} async-done(((bf16[4,512,1152]{2,1,0:T(8,128)(2,1)}), bf16[1,512,1152]{2,1,0:T(8,128)(2,1)}) %reduce-scatter.2.cloned.1.call-update) | async-done | bytes 1179664 | tf_op jit(solution)/shard_map/reduce_scatter | solution.py:87
  150.3 10.0 %all-to-all-start.1 = ((bf16[32,16,1152]{2,1,0:T(8,128)(2,1)}), bf16[32,16,1152]{2,1,0:T(8,128)(2,1)S(1)}, u32[]{:S(2)}, u32[]{:S(2)}) async-start(bf16[32,16,1152]{2,1,0:T(8,128)(2,1)} %bitcast.21), calls=%async_computation.2 | async-start | bytes 2359296 | tf_op jit(solution)/shard_map/all_to_all | solution.py:89
  160.4 30.9 %all-to-all-done.1 = bf16[32,16,1152]{2,1,0:T(8,128)(2,1)S(1)} async-done(((bf16[32,16,1152]{2,1,0:T(8,128)(2,1)}), bf16[32,16,1152]{2,1,0:T(8,128)(2,1)S(1)}, u32[]{:S(2)}, u32[]{:S(2)}) %all-to-all-start.1) | async-done | bytes 1179680 | tf_op jit(solution)/shard_map/all_to_all | solution.py:89
  191.3 3.4 %fusion.2 = bf16[1152,512]{1,0:T(8,128)(2,1)} fusion(s32[1152]{0:T(1024)S(1)} %fusion.29, bf16[512,1152]{1,0:T(8,128)(2,1)S(1)} %bitcast.22, s32[512]{0:T(512)S(1)} %fusion.38), kind=kOutput, calls=%fused_computation.4 | convolution fusion | flops 1965703168 | bytes 2365952 | tf_op jit(solution)/shard_map/dot_general | solution.py:97
  194.7 4.4 %all-to-all-start.2 = ((bf16[8,144,512]{2,1,0:T(8,128)(2,1)}), bf16[8,144,512]{2,1,0:T(8,128)(2,1)S(1)}, u32[]{:S(2)}, u32[]{:S(2)}) async-start(bf16[8,144,512]{2,1,0:T(8,128)(2,1)} %bitcast.13), calls=%async_computation.3 | async-start | bytes 2359296 | tf_op jit(solution)/shard_map/all_to_all | solution.py:100
  199.1 17.3 %all-to-all-done.2 = bf16[8,144,512]{2,1,0:T(8,128)(2,1)S(1)} async-done(((bf16[8,144,512]{2,1,0:T(8,128)(2,1)}), bf16[8,144,512]{2,1,0:T(8,128)(2,1)S(1)}, u32[]{:S(2)}, u32[]{:S(2)}) %all-to-all-start.2) | async-done | bytes 1179680 | tf_op jit(solution)/shard_map/all_to_all | solution.py:100
  216.5 3.2 %fusion.5 = bf16[512,1152]{1,0:T(8,128)(2,1)} fusion(bf16[1,512,1152]{2,1,0:T(8,128)(2,1)S(1)} %copy-done, pred[1152]{0:T(1024)(128)(4,1)S(1)} %fusion.20, pred[512]{0:T(512)(128)(4,1)S(1)} %get-tuple-element.6, pred[512]{0:T(512)(128)(4,1)S(1)} %get-tuple-element.5, bf16[1152,512]{1,0:T(8,128)(2,1)S(1)} %bitcast.23, s32[1152]{0:T(1024)S(1)} %fusion.26), kind=kOutput, calls=%fused_computation.10 | convolution fusion | flops 1363230720 | bytes 3545728 | tf_op jit(solution)/shard_map/dot_general | solution.py:103
  (15 shorter events, 0.2 us)
Async XLA Ops:
  6.5 70.9 %all-gather.2.cloned.1.call-start = ((), (), s32[]{:S(2)}) async-start(), calls=%async_computation.4 | async-start | bytes 5971968 | tf_op jit(solution)/shard_map/all_gather | solution.py:76
  7.3 143.1 %reduce-scatter.2.cloned.1.call-start = ((), (), s32[]{:S(2)}) async-start(), calls=%async_computation.5 | async-start | bytes 5898240 | tf_op jit(solution)/shard_map/reduce_scatter | solution.py:87
  30.2 27.8 %collective-permute-start = (bf16[4,288,512]{2,1,0:T(8,128)(2,1)S(1)}, bf16[4,288,512]{2,1,0:T(8,128)(2,1)S(1)}, u32[]{:S(2)}, u32[]{:S(2)}) collective-permute-start(bf16[4,288,512]{2,1,0:T(8,128)(2,1)S(1)} %all_to_all.15.refs_0_), channel_id=1, source_target_pairs={{0,2},{2,4},{4,6},{6,0},{1,3},{3,5},{5,7},{7,1},{8,10},{10,12},{12... | collective-permute-start | bytes 3538952 | tf_op jit(solution)/shard_map/ppermute | solution.py:59
  31.7 26.7 %collective-permute-start.1 = (bf16[4,288,512]{2,1,0:T(8,128)(2,1)S(1)}, bf16[4,288,512]{2,1,0:T(8,128)(2,1)S(1)}, u32[]{:S(2)}, u32[]{:S(2)}) collective-permute-start(bf16[4,288,512]{2,1,0:T(8,128)(2,1)S(1)} %all_to_all.15.refs_0_), channel_id=1, source_target_pairs={{0,6},{2,0},{4,2},{6,4},{1,7},{3,1},{5,3},{7,5},{8,14},{10,8},{12,... | collective-permute-start | bytes 3538952 | tf_op jit(solution)/shard_map/ppermute | solution.py:60
  58.1 14.5 %collective-permute-start.2 = (bf16[2,288,512]{2,1,0:T(8,128)(2,1)S(1)}, bf16[2,288,512]{2,1,0:T(8,128)(2,1)S(1)}, u32[]{:S(2)}, u32[]{:S(2)}) collective-permute-start(bf16[2,288,512]{2,1,0:T(8,128)(2,1)S(1)} %slice.18), channel_id=1, source_target_pairs={{0,2},{2,4},{4,6},{6,0},{1,3},{3,5},{5,7},{7,1},{8,10},{10,12},{12... | collective-permute-start | bytes 1769480 | tf_op jit(solution)/shard_map/ppermute | solution.py:61
  58.5 14.9 %collective-permute-start.3 = (bf16[2,288,512]{2,1,0:T(8,128)(2,1)S(1)}, bf16[2,288,512]{2,1,0:T(8,128)(2,1)S(1)}, u32[]{:S(2)}, u32[]{:S(2)}) collective-permute-start(bf16[2,288,512]{2,1,0:T(8,128)(2,1)S(1)} %slice.19), channel_id=1, source_target_pairs={{0,6},{2,0},{4,2},{6,4},{1,7},{3,1},{5,3},{7,5},{8,14},{10,8},{12,... | collective-permute-start | bytes 1769480 | tf_op jit(solution)/shard_map/ppermute | solution.py:62
  61.6 12.8 %collective-permute-start.4 = (bf16[4,288,512]{2,1,0:T(8,128)(2,1)S(1)}, bf16[4,288,512]{2,1,0:T(8,128)(2,1)}, u32[]{:S(2)}, u32[]{:S(2)}) collective-permute-start(bf16[4,288,512]{2,1,0:T(8,128)(2,1)S(1)} %all_to_all.15.refs_0_), channel_id=1, source_target_pairs={{0,1},{1,0},{2,3},{3,2},{4,5},{5,4},{6,7},{7,6},{8,9},{9,8},{10,11... | collective-permute-start | bytes 3538952 | tf_op jit(solution)/shard_map/ppermute | solution.py:82
  61.6 12.8 %collective-permute-start.5 = (bf16[4,288,512]{2,1,0:T(8,128)(2,1)S(1)}, bf16[4,288,512]{2,1,0:T(8,128)(2,1)}, u32[]{:S(2)}, u32[]{:S(2)}) collective-permute-start(bf16[4,288,512]{2,1,0:T(8,128)(2,1)S(1)} %collective-permute-done.refs_1_), channel_id=1, source_target_pairs={{0,1},{1,0},{2,3},{3,2},{4,5},{5,4},{6,7},{7,6},{8,9},{9,8},{10,11... | collective-permute-start | bytes 3538952 | tf_op jit(solution)/shard_map/ppermute | solution.py:82
  62.1 12.3 %collective-permute-start.6 = (bf16[4,288,512]{2,1,0:T(8,128)(2,1)S(1)}, bf16[4,288,512]{2,1,0:T(8,128)(2,1)}, u32[]{:S(2)}, u32[]{:S(2)}) collective-permute-start(bf16[4,288,512]{2,1,0:T(8,128)(2,1)S(1)} %collective-permute-done.1.refs_2_), channel_id=1, source_target_pairs={{0,1},{1,0},{2,3},{3,2},{4,5},{5,4},{6,7},{7,6},{8,9},{9,8},{10,11... | collective-permute-start | bytes 3538952 | tf_op jit(solution)/shard_map/ppermute | solution.py:82
  74.3 3.2 %collective-permute-start.7 = (bf16[4,288,512]{2,1,0:T(8,128)(2,1)}, bf16[4,288,512]{2,1,0:T(8,128)(2,1)}, u32[]{:S(2)}, u32[]{:S(2)}) collective-permute-start(bf16[4,288,512]{2,1,0:T(8,128)(2,1)} %constant_dynamic-update-slice_fusion.refs_3_), channel_id=1, source_target_pairs={{0,1},{1,0},{2,3},{3,2},{4,5},{5,4},{6,7},{7,6},{8,9},{9,8},{10,11... | collective-permute-start | bytes 3538952 | tf_op jit(solution)/shard_map/ppermute | solution.py:82
  150.3 10.1 %copy-start.1 = (s32[512]{0:T(512)S(1)}, s32[512]{0:T(512)}, u32[]{:S(2)}) copy-start(s32[512]{0:T(512)} %param.7) | copy-start | bytes 6148
  150.3 40.9 %all-to-all-start.1 = ((bf16[32,16,1152]{2,1,0:T(8,128)(2,1)}), bf16[32,16,1152]{2,1,0:T(8,128)(2,1)S(1)}, u32[]{:S(2)}, u32[]{:S(2)}) async-start(bf16[32,16,1152]{2,1,0:T(8,128)(2,1)} %bitcast.21), calls=%async_computation.2 | async-start | bytes 2359296 | tf_op jit(solution)/shard_map/all_to_all | solution.py:89
  194.7 21.8 %copy-start = (bf16[1,512,1152]{2,1,0:T(8,128)(2,1)S(1)}, bf16[1,512,1152]{2,1,0:T(8,128)(2,1)}, u32[]{:S(2)}) copy-start(bf16[1,512,1152]{2,1,0:T(8,128)(2,1)} %reduce-scatter.2.cloned.1.call-done) | copy-start | bytes 3538948
  194.7 21.7 %all-to-all-start.2 = ((bf16[8,144,512]{2,1,0:T(8,128)(2,1)}), bf16[8,144,512]{2,1,0:T(8,128)(2,1)S(1)}, u32[]{:S(2)}, u32[]{:S(2)}) async-start(bf16[8,144,512]{2,1,0:T(8,128)(2,1)} %bitcast.13), calls=%async_computation.3 | async-start | bytes 2359296 | tf_op jit(solution)/shard_map/all_to_all | solution.py:100
Sparse Core Ops, SparseCore 0:
  9.1 68.1 all-gather.1
  97.0 53.2 reduce-scatter.1
